TPU v7x, 32 devices: a whole 2x2x4 slice. The times are simulated.
32 devices in a mesh: blocks: 2 (over y), rows: 4 (over z), cols: 4 (over x, core).
Axes of the slice: x: 2, y: 2, z: 4, core: 2. Of those that a mesh axis runs over, the one named last changes fastest.
Arguments:
- sens_tiles: bfloat16 [128, 1024, 256], P(('blocks', 'rows'), 'cols'), parts along dimension 0, may hold values from -10.606602 to 10.606602, as said below
- tile_coords: int32 [128, 8], P(('blocks', 'rows'), 'cols'), parts along dimension 0, may hold values from 0 to 7, as said below
- tile_counts: int32 [8, 4], P(('blocks', 'rows'), 'cols'), parts along dimension 0, may hold values from 3 to 16, as said below
- data_vec: float32 [192, 4096], P('blocks', 'rows'), parts along dimension 0, may hold values from -6 to 6
- cell_vec: float32 [192, 8192], P('blocks', 'cols'), parts along dimension 0, may hold values from -6 to 6
- alpha_now: float32 [192], P('blocks'), parts along dimension 0, may hold values from 0.5 to 2
Outputs:
- data_next: float32 [192, 4096], P('blocks', 'rows'), parts along dimension 0
- cell_next: float32 [192, 8192], P('blocks', 'cols'), parts along dimension 0
- beta_next: float32 [192], P('blocks'), parts along dimension 0
- alpha_next: float32 [192], P('blocks'), parts along dimension 0
There are 2 independent parts, one for each index of `blocks`. A program takes and returns all parts, laid end to end along the dimension named above; each array names one. Nothing has to cross between parts.
Inputs may be any that keep to these rules, and one draw needn't show every extreme that they name: `sens_tiles`: entries of the tiles; slots at or beyond a device's count hold values that belong to no tile. `tile_coords`: within one device all 16 slots name distinct (row tile, column tile) pairs; the first entry of a pair is below 4, the second below 8. `tile_counts`: every data-row band has one device whose count is 16.
All inputs are finite; a program needn't handle non-finite values.
Results may differ from a plain program's by a relative error of at most 0.0043.
Values sent between devices are 32-bit elements; how exact they have to be, the bound alone decides.
A program may use at most 64 MiB of HBM per device.

v0:
```python
import jax
import jax.numpy as jnp
from jax import lax
from jax.sharding import PartitionSpec as P

EPSILON = 1e-06


def listed_mask(sens_tiles, listed_count):
    return (jnp.arange(sens_tiles.shape[0], dtype=jnp.int32) < listed_count).astype(jnp.float32)


def forward_sweep(sens_tiles, tile_coords, listed_count, cell_low, row_tiles):
    samples = cell_low.shape[0]
    tile_size = sens_tiles.shape[1]
    listed = listed_mask(sens_tiles, listed_count)
    blocks = cell_low.reshape(samples, cell_low.shape[1] // tile_size, tile_size)
    picked = jnp.take(blocks, tile_coords[:, 1], axis=1)
    contrib = jnp.einsum("ktj,tij->kti", picked, sens_tiles, preferred_element_type=jnp.float32)
    spread = jax.nn.one_hot(tile_coords[:, 0], row_tiles, dtype=jnp.float32) * listed[:, None]
    placed = jnp.einsum("kti,tr->kri", contrib, spread, precision=lax.Precision.HIGHEST)
    return placed.reshape(samples, row_tiles * tile_size)


def adjoint_sweep(sens_tiles, tile_coords, listed_count, data_low, col_tiles):
    samples = data_low.shape[0]
    tile_size = sens_tiles.shape[1]
    listed = listed_mask(sens_tiles, listed_count)
    blocks = data_low.reshape(samples, data_low.shape[1] // tile_size, tile_size)
    picked = jnp.take(blocks, tile_coords[:, 0], axis=1)
    contrib = jnp.einsum("kti,tij->ktj", picked, sens_tiles, preferred_element_type=jnp.float32)
    spread = jax.nn.one_hot(tile_coords[:, 1], col_tiles, dtype=jnp.float32) * listed[:, None]
    placed = jnp.einsum("ktj,ts->ksj", contrib, spread, precision=lax.Precision.HIGHEST)
    return placed.reshape(samples, col_tiles * tile_size)


def per_device(sens_tiles, tile_coords, tile_counts, data_vec, cell_vec, alpha_now):
    tile_size = sens_tiles.shape[1]
    row_tiles = data_vec.shape[1] // tile_size
    col_tiles = cell_vec.shape[1] // tile_size
    listed_count = tile_counts[0, 0]
    data_total = data_vec.shape[1] * lax.axis_size("rows")
    cell_total = cell_vec.shape[1] * lax.axis_size("cols")
    cell_low = cell_vec.astype(jnp.bfloat16)
    partial_rows = forward_sweep(sens_tiles, tile_coords, listed_count, cell_low, row_tiles)
    row_full = lax.psum(partial_rows, "cols")
    residual = row_full - alpha_now[:, None] * data_vec
    squares = lax.psum(jnp.sum(residual * residual, axis=1), "rows")
    beta_next = jnp.sqrt(squares / data_total + EPSILON)
    data_next = residual / beta_next[:, None]
    data_low = data_next.astype(jnp.bfloat16)
    partial_cells = adjoint_sweep(sens_tiles, tile_coords, listed_count, data_low, col_tiles)
    cell_full = lax.psum(partial_cells, "rows")
    fresh = cell_full - beta_next[:, None] * cell_vec
    sumsq = lax.psum(jnp.sum(fresh * fresh, axis=1), "cols")
    alpha_next = jnp.sqrt(sumsq / cell_total + EPSILON)
    cell_next = fresh / alpha_next[:, None]
    return (data_next, cell_next, beta_next, alpha_next)


def solution(mesh):
    placed = (
        P(("blocks", "rows"), "cols", None),
        P(("blocks", "rows"), "cols"),
        P(("blocks", "rows"), "cols"),
        P("blocks", "rows"),
        P("blocks", "cols"),
        P("blocks"),
    )
    return jax.shard_map(
        per_device,
        mesh=mesh,
        in_specs=placed,
        out_specs=(P("blocks", "rows"), P("blocks", "cols"), P("blocks"), P("blocks")),
        check_vma=False,
    )
```

profile of v0, /device:TPU:0, one launch (start us, length us, event | category | flops | bytes accessed | tf_op | source)
XLA Modules:
  0.0 127.0 jit_solution(8777433551403314318)
XLA Ops:
  7.2 0.0 copy-start
  7.2 0.0 all-reduce.3.cloned.1.call-start
  7.2 0.8 and_bitcast_fusion
  8.1 0.8 slice_bitcast_fusion
  9.5 1.2 convert_element_type.19
  10.7 0.6 gather_fusion
  11.3 0.0 copy-done
  11.3 0.8 convolution_bitcast_fusion.1
  12.1 0.0 copy-start.2
  12.1 0.0 copy-start.4
  12.1 1.7 %fusion.2 = f32[4,96,256]{2,0,1:T(4,128)S(1)} fusion(f32[96,16,256]{2,0,1:T(8,128)S(1)} %convolution_bitcast_fusion.1, f32[16]{0:T(128)S(1)} %compare_convert_fusion, s32[16]{0:T(128)S(1)} %get-tuple-element.9), kind=kOutput, calls=%fused_computation.4 | convolution fusion | flops 18874496 | bytes 1966208 | tf_op jit(solution)/shard_map/kti,tr->kri/dot_general | solution.py:21
  13.9 0.8 copy.16
  14.7 0.0 all-reduce.3.cloned.1.call-update
  14.7 0.0 all-reduce.5.cloned.1.call-start
  14.8 35.4 %all-reduce.3.cloned.1.call-done = f32[96,1024]{1,0:T(8,128)} async-done(((f32[96,1024]{1,0:T(8,128)}), f32[96,1024]{1,0:T(8,128)}) %all-reduce.3.cloned.1.call-update) | async-done | bytes 393232 | tf_op jit(solution)/shard_map/psum | solution.py:46
  50.1 0.0 copy-done.2
  50.1 0.0 copy-done.4
  50.1 1.2 multiply_reduce_fusion.1
  51.4 11.7 %psum.29 = f32[96]{0:T(128)S(1)} all-reduce(f32[96]{0:T(128)S(1)} %multiply_reduce_fusion.1), channel_id=1, replica_groups=mesh['blocks'=2,'rows'=4,'cols'=4] {'rows'}, use_global_device_ids=true, to_apply=%region_2.3 | all-reduce | flops 96 | bytes 768 | tf_op jit(solution)/shard_map/psum | solution.py:48
  63.1 1.9 %fusion.28 = (bf16[96,1024]{1,0:T(8,128)(2,1)S(1)}, f32[96,1024]{1,0:T(8,128)}) fusion(f32[96]{0:T(128)S(1)} %add_sqrt_fusion.1, f32[96,1024]{1,0:T(8,128)} %all-reduce.3.cloned.1.call-done, f32[96,1024]{1,0:T(8,128)S(1)} %copy-done.2, f32[96]{0:T(128)S(1)} %copy-done.4), kind=kLoop, calls=%fused_computation.53 | loop fusion | flops 393216 | bytes 1377024 | tf_op jit(solution)/shard_map/convert_element_type | solution.py:51
  65.0 0.6 gather_fusion.1
  65.6 0.5 convolution_bitcast_fusion
  66.1 1.7 %fusion = f32[8,96,256]{2,0,1:T(8,128)S(1)} fusion(f32[96,16,256]{2,0,1:T(8,128)S(1)} %convolution_bitcast_fusion, f32[16]{0:T(128)S(1)} %compare_convert_fusion, s32[16]{0:T(128)S(1)} %get-tuple-element.6), kind=kOutput, calls=%fused_computation.2 | convolution fusion | flops 37748992 | bytes 2359424 | tf_op jit(solution)/shard_map/ktj,ts->ksj/dot_general | solution.py:33
  67.8 0.0 copy-start.1
  67.8 1.1 copy.17
  69.0 0.0 all-reduce.5.cloned.1.call-update
  69.0 41.1 %all-reduce.5.cloned.1.call-done = f32[96,2048]{1,0:T(8,128)} async-done(((f32[96,2048]{1,0:T(8,128)}), f32[96,2048]{1,0:T(8,128)}) %all-reduce.5.cloned.1.call-update) | async-done | bytes 786448 | tf_op jit(solution)/shard_map/psum | solution.py:53
  110.0 0.0 copy-done.1
  110.1 1.4 %multiply_reduce_fusion = f32[96]{0:T(128)S(1)} fusion(f32[96,2048]{1,0:T(8,128)} %all-reduce.5.cloned.1.call-done, f32[96,2048]{1,0:T(8,128)S(1)} %copy-done.1, f32[96]{0:T(128)S(1)} %add_sqrt_fusion.1), kind=kLoop, calls=%fused_computation.12 | loop fusion | flops 786336 | bytes 1573632 | tf_op jit(solution)/shard_map/reduce_sum | solution.py:55
  111.5 6.5 %psum.31 = f32[96]{0:T(128)S(1)} all-reduce(f32[96]{0:T(128)S(1)} %multiply_reduce_fusion), channel_id=1, replica_groups=mesh['blocks'=2,'rows'=4,'cols'=4] {'cols'}, use_global_device_ids=true, to_apply=%region_5.6 | all-reduce | flops 96 | bytes 768 | tf_op jit(solution)/shard_map/psum | solution.py:55
  118.0 0.0 copy-done.3
  118.0 2.2 %broadcast_divide_fusion = f32[96,2048]{1,0:T(8,128)} fusion(f32[96]{0:T(128)S(1)} %add_sqrt_fusion, f32[96,2048]{1,0:T(8,128)} %all-reduce.5.cloned.1.call-done, f32[96,2048]{1,0:T(8,128)S(1)} %copy-done.1, f32[96]{0:T(128)S(1)} %add_sqrt_fusion.1), kind=kLoop, calls=%fused_computation.19 | loop fusion | flops 589824 | bytes 2360064 | tf_op jit(solution)/shard_map/div | solution.py:57
  (9 shorter events, 0.1 us)
Async XLA Ops:
  7.2 4.2 %copy-start = (bf16[16,256,256]{2,1,0:T(8,128)(2,1)S(1)}, bf16[16,256,256]{2,1,0:T(8,128)(2,1)}, u32[]{:S(2)}) copy-start(bf16[16,256,256]{2,1,0:T(8,128)(2,1)} %param.6) | copy-start | bytes 6291460
  7.2 43.0 %all-reduce.3.cloned.1.call-start = ((), (), s32[]{:S(2)}) async-start(), calls=%async_computation | async-start | bytes 786432 | tf_op jit(solution)/shard_map/psum | solution.py:46
  12.1 38.0 %copy-start.2 = (f32[96,1024]{1,0:T(8,128)S(1)}, f32[96,1024]{1,0:T(8,128)}, u32[]{:S(2)}) copy-start(f32[96,1024]{1,0:T(8,128)} %param.9) | copy-start | bytes 1179652
  12.1 38.0 %copy-start.4 = (f32[96]{0:T(128)S(1)}, f32[96]{0:T(128)}, u32[]{:S(2)}) copy-start(f32[96]{0:T(128)} %param.11) | copy-start | bytes 1156
  14.7 95.3 %all-reduce.5.cloned.1.call-start = ((), (), s32[]{:S(2)}) async-start(), calls=%async_computation.1 | async-start | bytes 1572864 | tf_op jit(solution)/shard_map/psum | solution.py:53
  63.1 54.9 %copy-start.3 = (f32[96]{0:T(128)}, f32[96]{0:T(128)S(1)}, u32[]{:S(2)}) copy-start(f32[96]{0:T(128)S(1)} %add_sqrt_fusion.1) | copy-start | bytes 1156
  67.8 42.2 %copy-start.1 = (f32[96,2048]{1,0:T(8,128)S(1)}, f32[96,2048]{1,0:T(8,128)}, u32[]{:S(2)}) copy-start(f32[96,2048]{1,0:T(8,128)} %param.10) | copy-start | bytes 2359300
  118.0 2.2 %copy-start.5 = (f32[96]{0:T(128)}, f32[96]{0:T(128)S(1)}, u32[]{:S(2)}) copy-start(f32[96]{0:T(128)S(1)} %add_sqrt_fusion) | copy-start | bytes 1156
Sparse Core Ops, SparseCore 0:
  14.8 35.2 all-reduce.2
  69.1 40.9 all-reduce.4
where the time goes:
time: 127 us
  waiting for transfers between devices  76.5 us (60%)
  blocking collectives  18.2 us (14%)
  between operations  14.8 us (12%)
  other arithmetic  9.5 us (7%)
  matrix products  4.7 us (4%)
  local copies, waits for them, and re-layouts  3.22 us (3%)
    psum x1, waiting for transfers between devices, per_device(): cell_full = lax.psum(partial_cells, 'rows')  41.1 us
    psum x1, waiting for transfers between devices, per_device(): row_full = lax.psum(partial_rows, 'cols')  35.4 us
    psum x1, blocking collectives, per_device(): squares = lax.psum(jnp.sum(residual * residual, axis=1), 'rows')  11.7 us
    psum x1, blocking collectives, per_device(): sumsq = lax.psum(jnp.sum(fresh * fresh, axis=1), 'cols')  6.48 us
  transfers between devices with their start and end apart: 2, of which 2 were waited for; matrix products, arithmetic and copies ran while one was open for 0% of the time, Pallas kernels for 0%

commit v1 on v0

v1 whole, which is shorter than its diff:
```python
import functools

import jax
import jax.numpy as jnp
from jax import lax
from jax.experimental import pallas as pl
from jax.experimental.pallas import tpu as pltpu
from jax.sharding import PartitionSpec as P

EPSILON = 1e-06
MESH = pl.DeviceIdType.MESH
CHUNK = 256


def remote(src, dst, send_sem, recv_sem, axis, peer):
    return pltpu.make_async_remote_copy(
        src_ref=src, dst_ref=dst, send_sem=send_sem, recv_sem=recv_sem, device_id={axis: peer}, device_id_type=MESH
    )


class Line:
    def __init__(self, count, place, axis, device_of, own, up, down, up_out, down_out, sems):
        self.count, self.place, self.axis, self.device_of = count, place, axis, device_of
        self.own, self.up, self.down, self.up_out, self.down_out = own, up, down, up_out, down_out
        self.up_send, self.up_recv, self.down_send, self.down_recv = sems
        self.chunks = own.shape[0]

    def up_copy(self, src, i):
        peer = self.device_of(lax.rem(self.place + 1, self.count))
        return remote(src.at[i], self.up.at[i], self.up_send.at[i], self.up_recv.at[i], self.axis, peer)

    def down_copy(self, src, i):
        peer = self.device_of(lax.rem(self.place + self.count - 1, self.count))
        return remote(src.at[i], self.down.at[i], self.down_send.at[i], self.down_recv.at[i], self.axis, peer)

    def begin(self, i):
        @pl.when(self.place == 0)
        def _():
            self.up_copy(self.own, i).start()

        @pl.when(self.place == self.count - 1)
        def _():
            self.down_copy(self.own, i).start()

    def run(self, finish):
        first, last = self.place == 0, self.place == self.count - 1
        from_below = self.place
        from_above = self.count - 1 - self.place

        def slot(s, carry):
            i = s - from_below

            @pl.when(jnp.logical_not(first) & (i >= 0) & (i < self.chunks))
            def _():
                self.up_copy(self.up_out, i).wait_recv()

                @pl.when(jnp.logical_not(last))
                def _():
                    self.up_out[i] = self.own[i] + self.up[i]
                    self.up_copy(self.up_out, i).start()

            k = s - from_above

            @pl.when(jnp.logical_not(last) & (k >= 0) & (k < self.chunks))
            def _():
                self.down_copy(self.down_out, k).wait_recv()

                @pl.when(jnp.logical_not(first))
                def _():
                    self.down_out[k] = self.own[k] + self.down[k]
                    self.down_copy(self.down_out, k).start()

            m = s - jnp.maximum(from_below, from_above)

            @pl.when((m >= 0) & (m < self.chunks))
            def _():
                @pl.when(first)
                def _():
                    finish(m, self.own[m] + self.down[m])

                @pl.when(last)
                def _():
                    finish(m, self.up[m] + self.own[m])

                if self.count > 2:

                    @pl.when(jnp.logical_not(first | last))
                    def _():
                        finish(m, self.up_out[m] + self.down[m])

            return carry

        lax.fori_loop(0, self.chunks + self.count - 1, slot, 0)

    def end(self):
        def one(i, carry):
            @pl.when(self.place < self.count - 1)
            def _():
                self.up_copy(self.own, i).wait_send()

            @pl.when(self.place > 0)
            def _():
                self.down_copy(self.own, i).wait_send()

            return carry

        lax.fori_loop(0, self.chunks, one, 0)


def share_start(axis, count, me, row, out, got, send, recv):
    wide = jnp.broadcast_to(row, out.shape)
    out[...] = wide
    got[me] = wide

    def one(d, carry):
        peer = lax.rem(me + d, count)
        remote(out, got.at[me], send.at[d], recv.at[me], axis, peer).start()
        return carry

    lax.fori_loop(1, count, one, 0)


def share_end(axis, count, me, out, got, send, recv):
    def one(d, carry):
        peer = lax.rem(me + d, count)
        remote(out, got.at[peer], send.at[d], recv.at[peer], axis, peer).wait_recv()
        return carry

    lax.fori_loop(1, count, one, 0)

    def sent(d, carry):
        peer = lax.rem(me + d, count)
        remote(out, got.at[me], send.at[d], recv.at[me], axis, peer).wait_send()
        return carry

    lax.fori_loop(1, count, sent, 0)
    total = got[0]
    for j in range(1, count):
        total = total + got[j]
    return total[0:1]


def kernel(
    rows, cols,
    coords, counts, alpha_in, tiles_in, data_in, cell_in,
    data_out, cell_out, beta_out, alpha_out,
    table, keys, tiles, data, cell, cell_low, other, other_got, half, half_up, half_down, half_up_out, half_down_out,
    resid, resid_low, part, part_up, part_down, part_up_out, part_down_out, squares,
    beta_row, beta_got, alpha_row, alpha_got,
    load_sems, pair_send, pair_recv, back_send, back_recv, half_sems, part_sems, beta_sems, alpha_sems,
):
    slots, tile = tiles_in.shape[0], tiles_in.shape[1]
    samples = data_in.shape[0]
    row_tiles, col_tiles = data_in.shape[1] // tile, cell_in.shape[1] // tile
    halves = row_tiles // 2
    r, c = lax.axis_index("rows"), lax.axis_index("cols")
    side = lax.rem(c, 2)
    group = c // 2
    partner = c + 1 - 2 * side

    barrier = pltpu.get_barrier_semaphore()

    def greet(axis, count, me):
        def one(d, carry):
            pl.semaphore_signal(barrier, inc=1, device_id={axis: lax.rem(me + d, count)}, device_id_type=MESH)
            return carry

        lax.fori_loop(1, count, one, 0)

    greet("rows", rows, r)
    greet("cols", cols, c)

    loads = [
        pltpu.make_async_copy(cell_in, cell, load_sems.at[0]),
        pltpu.make_async_copy(tiles_in, tiles.at[pl.ds(0, slots)], load_sems.at[1]),
        pltpu.make_async_copy(data_in, data, load_sems.at[2]),
    ]
    for load in loads:
        load.start()
    tiles[slots] = jnp.zeros(tiles.shape[1:], tiles.dtype)

    listed = counts[0, 0]
    for t in range(slots):
        keys[t] = jnp.where(t < listed, coords[t, 0] * col_tiles + coords[t, 1], -1)

    def find(p, carry):
        found = jnp.int32(slots)
        for t in range(slots):
            found = jnp.where(keys[t] == p, t, found)
        table[p] = found
        return carry

    lax.fori_loop(0, row_tiles * col_tiles, find, 0)

    lanes = alpha_in.shape[1]
    eye = lax.broadcasted_iota(jnp.int32, (samples, lanes), 0) == lax.broadcasted_iota(jnp.int32, (samples, lanes), 1)

    def as_row(column):
        return jnp.sum(jnp.where(eye, column, 0.0), axis=0, keepdims=True)

    def as_column(row):
        return jnp.sum(jnp.where(eye, row, 0.0), axis=1, keepdims=True)

    alpha = as_column(alpha_in[...])

    loads[0].wait()
    for b in range(col_tiles):
        cell_low[b] = cell[:, b * tile:(b + 1) * tile].astype(jnp.bfloat16)
    loads[1].wait()

    def forward(a):
        total = None
        for b in range(col_tiles):
            term = lax.dot_general(
                cell_low[b], tiles[table[a * col_tiles + b]], (((1,), (1,)), ((), ())),
                preferred_element_type=jnp.float32,
            )
            total = term if total is None else total + term
        return total

    def pair_copy(j):
        return remote(other.at[j], other_got.at[j], pair_send.at[j], pair_recv.at[j], "cols", partner)

    other[0] = forward((1 - side) * halves)
    pl.semaphore_wait(barrier, rows + cols - 2)
    pair_copy(0).start()
    for j in range(1, halves):
        other[j] = forward((1 - side) * halves + j)
        pair_copy(j).start()

    across = Line(
        cols // 2, group, "cols", lambda q: q * 2 + side, half, half_up, half_down, half_up_out, half_down_out,
        [half_sems.at[i] for i in range(4)],
    )
    for j in range(halves):
        own = forward(side * halves + j)
        pair_copy(j).wait_recv()
        half[j] = own + other_got[j]
        across.begin(j)

    loads[2].wait()

    def back_copy(a, j):
        return remote(resid.at[a], resid.at[a], back_send.at[j], back_recv.at[j], "cols", partner)

    def finish_rows(j, total):
        a = side * halves + j
        here = pl.ds(pl.multiple_of(a * tile, tile), tile)
        resid[a] = total - alpha * data[:, here]
        back_copy(a, j).start()

    across.run(finish_rows)
    for j in range(halves):
        back_copy((1 - side) * halves + j, j).wait_recv()

    sums = jnp.zeros((samples, 1), jnp.float32)
    for a in range(row_tiles):
        block = resid[a]
        resid_low[a] = block.astype(jnp.bfloat16)
        sums = sums + jnp.sum(block * block, axis=1, keepdims=True)
    share_start("rows", rows, r, as_row(sums), beta_row, beta_got, beta_sems.at[0], beta_sems.at[1])

    along = Line(
        rows, r, "rows", lambda q: q, part, part_up, part_down, part_up_out, part_down_out,
        [part_sems.at[i] for i in range(4)],
    )
    width = part.shape[2]
    pieces = tile // width
    for b in range(col_tiles):
        total = None
        for a in range(row_tiles):
            term = jnp.dot(resid_low[a], tiles[table[a * col_tiles + b]], preferred_element_type=jnp.float32)
            total = term if total is None else total + term
        for e in range(pieces):
            part[b * pieces + e] = total[:, e * width:(e + 1) * width]
            along.begin(b * pieces + e)

    data_total = jnp.float32(data_in.shape[1] * rows)
    cell_total = jnp.float32(cell_in.shape[1] * cols)
    beta = jnp.sqrt(
        share_end("rows", rows, r, beta_row, beta_got, beta_sems.at[0], beta_sems.at[1]) / data_total + EPSILON
    )
    beta_out[...] = beta
    beta_column = as_column(beta)
    beta_inverse = 1.0 / beta_column
    for a in range(row_tiles):
        data_out[:, a * tile:(a + 1) * tile] = resid[a] * beta_inverse
    squares[...] = jnp.zeros_like(squares)

    def finish_cells(i, total):
        here = pl.ds(pl.multiple_of(i * width, width), width)
        fresh = total * beta_inverse - beta_column * cell[:, here]
        cell_out[:, here] = fresh
        square = fresh * fresh
        piece = square[:, :128]
        for e in range(1, width // 128):
            piece = piece + square[:, e * 128:(e + 1) * 128]
        squares[...] += piece

    along.run(finish_cells)
    sums = jnp.sum(squares[...], axis=1, keepdims=True)
    share_start("cols", cols, c, as_row(sums), alpha_row, alpha_got, alpha_sems.at[0], alpha_sems.at[1])
    for j in range(halves):
        pair_copy(j).wait_send()
        back_copy(side * halves + j, j).wait_send()
    across.end()
    along.end()
    alpha_next = jnp.sqrt(
        share_end("cols", cols, c, alpha_row, alpha_got, alpha_sems.at[0], alpha_sems.at[1]) / cell_total + EPSILON
    )
    alpha_out[...] = alpha_next
    alpha_inverse = 1.0 / as_column(alpha_next)
    for b in range(col_tiles):
        here = slice(b * tile, (b + 1) * tile)
        cell_out[:, here] = cell_out[:, here] * alpha_inverse


def per_device(rows, cols, sens_tiles, tile_coords, tile_counts, data_vec, cell_vec, alpha_now):
    slots, tile = sens_tiles.shape[0], sens_tiles.shape[1]
    samples, data_size = data_vec.shape
    cell_size = cell_vec.shape[1]
    row_tiles, col_tiles = data_size // tile, cell_size // tile
    halves = row_tiles // 2
    chunks = cell_size // CHUNK
    lanes = (samples + 127) // 128 * 128
    f32, bf16 = jnp.float32, jnp.bfloat16
    alpha_wide = jnp.pad(alpha_now, (0, lanes - samples)).reshape(1, lanes)
    half = pltpu.VMEM((halves, samples, tile), f32)
    part = pltpu.VMEM((chunks, samples, CHUNK), f32)
    dma = pltpu.SemaphoreType.DMA
    vmem = pl.BlockSpec(memory_space=pltpu.VMEM)
    smem = pl.BlockSpec(memory_space=pltpu.SMEM)
    hbm = pl.BlockSpec(memory_space=pl.ANY)
    data_next, cell_next, beta, alpha = pl.pallas_call(
        functools.partial(kernel, rows, cols),
        out_shape=(
            jax.ShapeDtypeStruct((samples, data_size), f32),
            jax.ShapeDtypeStruct((samples, cell_size), f32),
            jax.ShapeDtypeStruct((1, lanes), f32),
            jax.ShapeDtypeStruct((1, lanes), f32),
        ),
        in_specs=[smem, smem, vmem, hbm, hbm, hbm],
        out_specs=(vmem, vmem, vmem, vmem),
        scratch_shapes=[
            pltpu.SMEM((row_tiles * col_tiles,), jnp.int32),
            pltpu.SMEM((slots,), jnp.int32),
            pltpu.VMEM((slots + 1, tile, tile), bf16),
            pltpu.VMEM((samples, data_size), f32),
            pltpu.VMEM((samples, cell_size), f32),
            pltpu.VMEM((col_tiles, samples, tile), bf16),
            half, half, half, half, half, half, half,
            pltpu.VMEM((row_tiles, samples, tile), f32),
            pltpu.VMEM((row_tiles, samples, tile), bf16),
            part, part, part, part, part,
            pltpu.VMEM((samples, 128), f32),
            pltpu.VMEM((8, lanes), f32),
            pltpu.VMEM((rows, 8, lanes), f32),
            pltpu.VMEM((8, lanes), f32),
            pltpu.VMEM((cols, 8, lanes), f32),
            dma((3,)),
            dma((halves,)), dma((halves,)), dma((halves,)), dma((halves,)),
            dma((4, halves)),
            dma((4, chunks)),
            dma((2, rows)),
            dma((2, cols)),
        ],
        compiler_params=pltpu.CompilerParams(
            collective_id=0, has_side_effects=True, vmem_limit_bytes=40 * 2**20
        ),
    )(tile_coords, tile_counts, alpha_wide, sens_tiles, data_vec, cell_vec)
    return data_next, cell_next, beta[0, :samples], alpha[0, :samples]


def solution(mesh):
    placed = (
        P(("blocks", "rows"), "cols", None),
        P(("blocks", "rows"), "cols"),
        P(("blocks", "rows"), "cols"),
        P("blocks", "rows"),
        P("blocks", "cols"),
        P("blocks"),
    )
    return jax.shard_map(
        functools.partial(per_device, mesh.shape["rows"], mesh.shape["cols"]),
        mesh=mesh,
        in_specs=placed,
        out_specs=(P("blocks", "rows"), P("blocks", "cols"), P("blocks"), P("blocks")),
        check_vma=False,
    )
```

time: 127 us -> 58.8 us (0.46)
  waiting for transfers between devices: 76.5 us -> 0 us
  Pallas kernels: 0 us -> 50 us
  blocking collectives: 18.2 us -> 0 us
  between operations: 14.8 us -> 1.29 us
  other arithmetic: 9.5 us -> 0 us
  matrix products: 4.7 us -> 0 us
  local copies, waits for them, and re-layouts: 3.22 us -> 7.27 us
    psum x2 -> x0, waiting for transfers between devices: 76.5 us -> none  [the longest x1 41.1 us: per_device(): cell_full = lax.psum(partial_cells, 'rows')]
    pallas_call x0 -> x1, Pallas kernels: none -> 50 us  [per_device(): pl.pallas_call(functools.partial(kernel, rows, cols), out_shape=(jax.Shap...]
    psum x2 -> x0, blocking collectives: 18.2 us -> none  [the longest x1 11.7 us: per_device(): squares = lax.psum(jnp.sum(residual * residual, axis=1), 'rows')]
    dot_general x4 -> x0, matrix products: 4.7 us -> none  [the longest x1 1.71 us: adjoint_sweep(): jnp.einsum('ktj,ts->ksj', contrib, spread, precision=lax.Precision.HIGHEST)]
    unnamed x14 -> x9, local copies, waits for them, and re-layouts: 1.98 us -> 6.1 us
    convert_element_type x3 -> x0, other arithmetic: 3.06 us -> none  [the longest x1 1.88 us: per_device(): data_low = data_next.astype(jnp.bfloat16)]
    reduce_sum x2 -> x0, other arithmetic: 2.62 us -> none  [the longest x1 1.41 us: per_device(): sumsq = lax.psum(jnp.sum(fresh * fresh, axis=1), 'cols')]
    div x1 -> x0, other arithmetic: 2.18 us -> none  [per_device(): cell_next = fresh / alpha_next[:, None]]
  transfers between devices with their start and end apart: 2 -> 0, of which waited for: 2 -> 0; matrix products, arithmetic and copies ran while one was open for 0% -> 0% of each run, Pallas kernels for 0% -> 0%
where the time goes in v1:
time: 58.8 us; the launch traced here: 58.6 us
  Pallas kernels  50 us (85%)
  local copies, waits for them, and re-layouts  7.27 us (12%)
  between operations  1.29 us (2%)
    pallas_call x1, Pallas kernels, per_device(): pl.pallas_call(functools.partial(kernel, rows, cols), out_shape=(jax.Shap...  50 us
    unnamed x9, local copies, waits for them, and re-layouts  6.1 us

profile of v1, /device:TPU:0, one launch (start us, length us, event | category | flops | bytes accessed | tf_op | source)
XLA Modules:
  0.0 58.6 jit_solution(10122897096252717134)
XLA Ops:
  1.3 0.7 %pad_bitcast_fusion.alpha_in = f32[1,128]{1,0:T(1,128)S(1)} fusion(f32[96]{0:T(128)} %param.11), kind=kLoop, calls=%fused_computation.2 | loop fusion | bytes 896 | tf_op jit(solution)/shard_map/reshape | solution.py:327
  1.9 0.8 %copy.10.coords = s32[16,2]{1,0:T(8,128)S(1)} copy(s32[16,2]{0,1:T(2,128)} %param.7) | data formatting | bytes 256 | tf_op args[1]
  2.7 0.0 copy-start
  2.7 1.6 %copy-done = bf16[16,256,256]{2,1,0:T(8,128)(2,1)S(1)} copy-done((bf16[16,256,256]{2,1,0:T(8,128)(2,1)S(1)}, bf16[16,256,256]{2,1,0:T(8,128)(2,1)}, u32[]{:S(2)}) %copy-start) | copy-done | bytes 2097176
  4.3 0.0 copy-start.1
  4.3 1.1 %copy-done.1 = f32[96,2048]{1,0:T(8,128)S(1)} copy-done((f32[96,2048]{1,0:T(8,128)S(1)}, f32[96,2048]{1,0:T(8,128)}, u32[]{:S(2)}) %copy-start.1) | copy-done | bytes 786456
  5.4 0.0 copy-start.2
  5.4 1.0 %copy-done.2 = f32[96,1024]{1,0:T(8,128)S(1)} copy-done((f32[96,1024]{1,0:T(8,128)S(1)}, f32[96,1024]{1,0:T(8,128)}, u32[]{:S(2)}) %copy-start.2) | copy-done | bytes 393240
  6.4 50.0 %shard_map.93 = (f32[96,1024]{1,0:T(8,128)S(1)}, f32[96,2048]{1,0:T(8,128)S(1)}, f32[1,128]{1,0:T(1,128)S(1)}, f32[1,128]{1,0:T(1,128)S(1)}) custom-call(s32[16,2]{1,0:T(8,128)S(1)} %copy.10.coords, s32[1,1]{1,0:T(1,128)S(6)} %copy.13.counts, f32[1,128]{1,0:T(1,128)S(1)} %pad_bitcast_fusion.alpha_in, bf16[16,256,256]{2,1,0:T(8,128)(2,1)S(1)} %copy-done, ...), custom_call_target="tpu_custom_call" | custom-call | tf_op jit(solution)/shard_map/pallas_call | solution.py:334
  56.4 0.5 slice_bitcast_fusion
  56.9 0.7 %copy.14 = f32[96,1024]{1,0:T(8,128)} copy(f32[96,1024]{1,0:T(8,128)S(1)} %get-tuple-element.18) | data formatting | bytes 786432
  57.7 0.9 %copy.15 = f32[96,2048]{1,0:T(8,128)} copy(f32[96,2048]{1,0:T(8,128)S(1)} %get-tuple-element.19) | data formatting | bytes 1572864
Async XLA Ops:
  2.7 1.6 %copy-start = (bf16[16,256,256]{2,1,0:T(8,128)(2,1)S(1)}, bf16[16,256,256]{2,1,0:T(8,128)(2,1)}, u32[]{:S(2)}) copy-start(bf16[16,256,256]{2,1,0:T(8,128)(2,1)} %tiles_in.1) | copy-start | bytes 6291460
  4.3 1.1 %copy-start.1 = (f32[96,2048]{1,0:T(8,128)S(1)}, f32[96,2048]{1,0:T(8,128)}, u32[]{:S(2)}) copy-start(f32[96,2048]{1,0:T(8,128)} %cell_in.1) | copy-start | bytes 2359300
  5.4 1.0 %copy-start.2 = (f32[96,1024]{1,0:T(8,128)S(1)}, f32[96,1024]{1,0:T(8,128)}, u32[]{:S(2)}) copy-start(f32[96,1024]{1,0:T(8,128)} %data_in.1) | copy-start | bytes 1179652

commit v2 on v1

v2 whole, which is shorter than its diff:
```python
import functools

import jax
import jax.numpy as jnp
from jax import lax
from jax.experimental import pallas as pl
from jax.experimental.pallas import tpu as pltpu
from jax.sharding import PartitionSpec as P

EPSILON = 1e-06
MESH = pl.DeviceIdType.MESH
HOP = 5
GROUPS = 1
PIECES = 3
WINDOW = 4
LOADS = 4


def remote(src, dst, send_sem, recv_sem, axis, peer):
    return pltpu.make_async_remote_copy(
        src_ref=src, dst_ref=dst, send_sem=send_sem, recv_sem=recv_sem, device_id={axis: peer}, device_id_type=MESH
    )


class Line:
    def __init__(self, count, place, axis, device_of, own, up, down, up_out, down_out, sems, window=0):
        self.count, self.place, self.axis, self.device_of = count, place, axis, device_of
        self.own, self.up, self.down, self.up_out, self.down_out = own, up, down, up_out, down_out
        self.up_send, self.up_recv, self.down_send, self.down_recv = sems
        self.chunks, self.window = own.shape[0], window

    def up_copy(self, src, i):
        peer = self.device_of(lax.rem(self.place + 1, self.count))
        return remote(src.at[i], self.up.at[i], self.up_send.at[i], self.up_recv.at[i], self.axis, peer)

    def down_copy(self, src, i):
        peer = self.device_of(lax.rem(self.place + self.count - 1, self.count))
        return remote(src.at[i], self.down.at[i], self.down_send.at[i], self.down_recv.at[i], self.axis, peer)

    def begin(self, i):
        @pl.when(self.place == 0)
        def _():
            self.up_copy(self.own, i).start()

        @pl.when(self.place == self.count - 1)
        def _():
            self.down_copy(self.own, i).start()

    def paced(self, copy, i):
        if self.window:

            @pl.when(i >= self.window)
            def _():
                copy(self.own, i - self.window).wait_send()

    def run(self, low, high, spread, finish):
        first, last = self.place == 0, self.place == self.count - 1
        from_below = self.place * spread
        from_above = (self.count - 1 - self.place) * spread

        def slot(s, carry):
            i = low + s - from_below

            @pl.when((i >= low) & (i < high))
            def _():
                if self.window:

                    @pl.when(first)
                    def _():
                        self.paced(self.up_copy, i)
                        self.up_copy(self.own, i).start()

                @pl.when(jnp.logical_not(first))
                def _():
                    self.up_copy(self.up_out, i).wait_recv()

                    @pl.when(jnp.logical_not(last))
                    def _():
                        self.up_out[i] = self.own[i] + self.up[i]
                        self.paced(self.up_copy, i)
                        self.up_copy(self.up_out, i).start()

            k = low + s - from_above

            @pl.when((k >= low) & (k < high))
            def _():
                if self.window:

                    @pl.when(last)
                    def _():
                        self.paced(self.down_copy, k)
                        self.down_copy(self.own, k).start()

                @pl.when(jnp.logical_not(last))
                def _():
                    self.down_copy(self.down_out, k).wait_recv()

                    @pl.when(jnp.logical_not(first))
                    def _():
                        self.down_out[k] = self.own[k] + self.down[k]
                        self.paced(self.down_copy, k)
                        self.down_copy(self.down_out, k).start()

            m = low + s - jnp.maximum(from_below, from_above)

            @pl.when((m >= low) & (m < high))
            def _():
                @pl.when(first)
                def _():
                    finish(m, self.own[m] + self.down[m])

                @pl.when(last)
                def _():
                    finish(m, self.up[m] + self.own[m])

                if self.count > 2:

                    @pl.when(jnp.logical_not(first | last))
                    def _():
                        finish(m, self.up_out[m] + self.down[m])

            return carry

        lax.fori_loop(0, high - low + (self.count - 1) * spread, slot, 0)

    def end(self):
        def one(i, carry):
            @pl.when(self.place < self.count - 1)
            def _():
                self.up_copy(self.own, i).wait_send()

            @pl.when(self.place > 0)
            def _():
                self.down_copy(self.own, i).wait_send()

            return carry

        lax.fori_loop(max(self.chunks - self.window, 0) if self.window else 0, self.chunks, one, 0)


def share_start(axis, count, me, row, out, got, send, recv):
    wide = jnp.broadcast_to(row, out.shape)
    out[...] = wide
    got[me] = wide

    def one(d, carry):
        peer = lax.rem(me + d, count)
        remote(out, got.at[me], send.at[d], recv.at[me], axis, peer).start()
        return carry

    lax.fori_loop(1, count, one, 0)


def share_end(axis, count, me, out, got, send, recv):
    def one(d, carry):
        peer = lax.rem(me + d, count)
        remote(out, got.at[peer], send.at[d], recv.at[peer], axis, peer).wait_recv()
        return carry

    lax.fori_loop(1, count, one, 0)

    def sent(d, carry):
        peer = lax.rem(me + d, count)
        remote(out, got.at[me], send.at[d], recv.at[me], axis, peer).wait_send()
        return carry

    lax.fori_loop(1, count, sent, 0)
    total = got[0]
    for j in range(1, count):
        total = total + got[j]
    return total[0:1]


def kernel(
    rows, cols, groups,
    coords, counts, alpha_in, tiles_in, data_in, cell_in,
    data_out, cell_out, beta_out, alpha_out,
    table, tiles, data, cell, cell_low, other, other_got, half, half_up, half_down, half_up_out, half_down_out,
    resid, part, part_up, part_down, part_up_out, part_down_out, squares, data_squares, beta_wide, inverse_wide,
    beta_row, beta_got, alpha_row, alpha_got,
    load_sems, pair_send, pair_recv, back_send, back_recv, half_sems, part_sems, beta_sems, alpha_sems,
):
    slots, tile = tiles_in.shape[0], tiles_in.shape[1]
    samples = data_in.shape[0]
    row_tiles, col_tiles = data_in.shape[1] // tile, cell_in.shape[1] // tile
    halves = row_tiles // 2
    size = samples // groups
    strip = size // PIECES
    r, c = lax.axis_index("rows"), lax.axis_index("cols")
    side = lax.rem(c, 2)
    group = c // 2
    partner = c + 1 - 2 * side

    barrier = pltpu.get_barrier_semaphore()

    def greet(axis, count, me):
        def one(d, carry):
            pl.semaphore_signal(barrier, inc=1, device_id={axis: lax.rem(me + d, count)}, device_id_type=MESH)
            return carry

        lax.fori_loop(1, count, one, 0)

    greet("rows", rows, r)
    greet("cols", cols, c)

    loads = [
        pltpu.make_async_copy(cell_in, cell, load_sems.at[0]),
        pltpu.make_async_copy(data_in, data, load_sems.at[1]),
    ]
    part_slots = slots // LOADS
    for e in range(LOADS):
        some = pl.ds(e * part_slots, part_slots)
        loads.append(pltpu.make_async_copy(tiles_in.at[some], tiles.at[some], load_sems.at[2 + e]))
    for load in loads:
        load.start()
    tiles[slots] = jnp.zeros(tiles.shape[1:], tiles.dtype)

    listed = counts[0, 0]
    keys = [jnp.where(t < listed, coords[0, t] * col_tiles + coords[1, t], -1) for t in range(slots)]

    def find(p, carry):
        found = jnp.int32(slots)
        for t in range(slots):
            found = jnp.where(keys[t] == p, t, found)
        table[p] = found
        return carry

    lax.fori_loop(0, row_tiles * col_tiles, find, 0)

    square = (samples, samples)
    eye = lax.broadcasted_iota(jnp.int32, square, 0) == lax.broadcasted_iota(jnp.int32, square, 1)

    def as_row(column):
        return jnp.sum(jnp.where(eye, column, 0.0), axis=0, keepdims=True)

    def as_column(row):
        return jnp.sum(jnp.where(eye, row, 0.0), axis=1, keepdims=True)

    def folded(block):
        piece = block[:, :128]
        for e in range(1, block.shape[1] // 128):
            piece = piece + block[:, e * 128:(e + 1) * 128]
        return piece

    alpha = as_column(alpha_in[...])
    squares[...] = jnp.zeros_like(squares)

    loads[0].wait()
    for b in range(col_tiles):
        cell_low[b] = cell[:, b * tile:(b + 1) * tile].astype(jnp.bfloat16)
    for load in loads[2:]:
        load.wait()

    across = Line(
        cols // 2, group, "cols", lambda q: q * 2 + side, half, half_up, half_down, half_up_out, half_down_out,
        [half_sems.at[i] for i in range(4)],
    )
    along = Line(
        rows, r, "rows", lambda q: q, part, part_up, part_down, part_up_out, part_down_out,
        [part_sems.at[i] for i in range(4)], WINDOW,
    )

    def span(g):
        return slice(g * size, (g + 1) * size)

    def forward(g, a):
        total = None
        for b in range(col_tiles):
            term = lax.dot_general(
                cell_low[b, span(g)], tiles[table[a * col_tiles + b]], (((1,), (1,)), ((), ())),
                preferred_element_type=jnp.float32,
            )
            total = term if total is None else total + term
        return total

    def pair_copy(i):
        return remote(other.at[i], other_got.at[i], pair_send.at[i], pair_recv.at[i], "cols", partner)

    def back_copy(g, a, i):
        here = resid.at[g * row_tiles + a]
        return remote(here, here, back_send.at[i], back_recv.at[i], "cols", partner)

    def multiply(g):
        for j in range(halves):
            i = g * halves + j
            other[i] = forward(g, (1 - side) * halves + j)
            if i == 0:
                pl.semaphore_wait(barrier, rows + cols - 2)
            pair_copy(i).start()
        for j in range(halves):
            half[g * halves + j] = forward(g, side * halves + j)

    def exchange(g):
        for j in range(halves):
            i = g * halves + j
            pair_copy(i).wait_recv()
            half[i] = half[i] + other_got[i]
            across.begin(i)

    def reduce(g):
        def finish(i, total):
            a = side * halves + i - g * halves
            here = pl.ds(pl.multiple_of(a * tile, tile), tile)
            resid[g * row_tiles + a] = total - alpha[span(g)] * data[span(g), here]
            back_copy(g, a, i).start()

        across.run(g * halves, (g + 1) * halves, 1, finish)

    def adjoin(g):
        for j in range(halves):
            back_copy(g, (1 - side) * halves + j, g * halves + j).wait_recv()
        low, sums = [], None
        for a in range(row_tiles):
            block = resid[g * row_tiles + a]
            low.append(block.astype(jnp.bfloat16))
            piece = folded(block * block)
            sums = piece if sums is None else sums + piece
        data_squares[span(g)] = sums
        for b in range(col_tiles):
            total = None
            for a in range(row_tiles):
                term = jnp.dot(low[a], tiles[table[a * col_tiles + b]], preferred_element_type=jnp.float32)
                total = term if total is None else total + term
            for e in range(PIECES):
                part[(g * col_tiles + b) * PIECES + e] = total[e * strip:(e + 1) * strip]

    multiply(0)
    if groups > 1:
        multiply(1)
    exchange(0)
    loads[1].wait()
    for g in range(groups):
        if g + 2 < groups:
            multiply(g + 2)
        if g + 1 < groups:
            exchange(g + 1)
        reduce(g)
        adjoin(g)

    sums = jnp.sum(data_squares[...], axis=1, keepdims=True)
    share_start("rows", rows, r, as_row(sums), beta_row, beta_got, beta_sems.at[0], beta_sems.at[1])

    data_total = jnp.float32(data_in.shape[1] * rows)
    cell_total = jnp.float32(cell_in.shape[1] * cols)

    def finish_cells(i, total):
        @pl.when(i == 0)
        def _():
            beta = jnp.sqrt(
                share_end("rows", rows, r, beta_row, beta_got, beta_sems.at[0], beta_sems.at[1]) / data_total + EPSILON
            )
            beta_out[...] = beta
            column = as_column(beta)
            beta_wide[...] = jnp.broadcast_to(column, beta_wide.shape)
            inverse_wide[...] = jnp.broadcast_to(1.0 / column, inverse_wide.shape)

        tiles_before, e = i // PIECES, lax.rem(i, PIECES)
        g, b = tiles_before // col_tiles, lax.rem(tiles_before, col_tiles)
        who = pl.ds(pl.multiple_of(g * size + e * strip, strip), strip)
        for q in range(tile // 128):
            here = pl.ds(pl.multiple_of(b * tile + q * 128, 128), 128)
            fresh = total[:, q * 128:(q + 1) * 128] * inverse_wide[who] - beta_wide[who] * cell[who, here]
            cell_out[who, here] = fresh
            squares[who] += fresh * fresh

    along.run(0, groups * col_tiles * PIECES, HOP, finish_cells)
    sums = jnp.sum(squares[...], axis=1, keepdims=True)
    share_start("cols", cols, c, as_row(sums), alpha_row, alpha_got, alpha_sems.at[0], alpha_sems.at[1])
    for g in range(groups):
        for a in range(row_tiles):
            inverse = inverse_wide[span(g), :1]
            data_out[span(g), a * tile:(a + 1) * tile] = resid[g * row_tiles + a] * inverse
    for g in range(groups):
        for j in range(halves):
            pair_copy(g * halves + j).wait_send()
            back_copy(g, side * halves + j, g * halves + j).wait_send()
    across.end()
    along.end()
    alpha_next = jnp.sqrt(
        share_end("cols", cols, c, alpha_row, alpha_got, alpha_sems.at[0], alpha_sems.at[1]) / cell_total + EPSILON
    )
    alpha_out[...] = alpha_next
    alpha_inverse = 1.0 / as_column(alpha_next)
    for b in range(col_tiles):
        here = slice(b * tile, (b + 1) * tile)
        cell_out[:, here] = cell_out[:, here] * alpha_inverse


def per_device(rows, cols, sens_tiles, tile_coords, tile_counts, data_vec, cell_vec, alpha_now):
    slots, tile = sens_tiles.shape[0], sens_tiles.shape[1]
    samples, data_size = data_vec.shape
    cell_size = cell_vec.shape[1]
    row_tiles, col_tiles = data_size // tile, cell_size // tile
    halves = row_tiles // 2
    groups = next(g for g in (GROUPS, 2, 1) if samples % (16 * g) == 0 or g == 1)
    size = samples // groups
    f32, bf16 = jnp.float32, jnp.bfloat16
    half = pltpu.VMEM((groups * halves, size, tile), f32)
    part = pltpu.VMEM((groups * col_tiles * PIECES, size // PIECES, tile), f32)
    column = pltpu.VMEM((samples, 128), f32)
    dma = pltpu.SemaphoreType.DMA
    pairs = dma((groups * halves,))
    vmem = pl.BlockSpec(memory_space=pltpu.VMEM)
    smem = pl.BlockSpec(memory_space=pltpu.SMEM)
    hbm = pl.BlockSpec(memory_space=pltpu.HBM)
    data_next, cell_next, beta, alpha = pl.pallas_call(
        functools.partial(kernel, rows, cols, groups),
        out_shape=(
            jax.ShapeDtypeStruct((samples, data_size), f32),
            jax.ShapeDtypeStruct((samples, cell_size), f32),
            jax.ShapeDtypeStruct((1, samples), f32),
            jax.ShapeDtypeStruct((1, samples), f32),
        ),
        in_specs=[smem, smem, vmem, hbm, hbm, hbm],
        out_specs=(vmem, vmem, vmem, vmem),
        scratch_shapes=[
            pltpu.SMEM((row_tiles * col_tiles,), jnp.int32),
            pltpu.VMEM((slots + 1, tile, tile), bf16),
            pltpu.VMEM((samples, data_size), f32),
            pltpu.VMEM((samples, cell_size), f32),
            pltpu.VMEM((col_tiles, samples, tile), bf16),
            half, half, half, half, half, half, half,
            pltpu.VMEM((groups * row_tiles, size, tile), f32),
            part, part, part, part, part,
            column, column, column, column,
            pltpu.VMEM((8, samples), f32),
            pltpu.VMEM((rows, 8, samples), f32),
            pltpu.VMEM((8, samples), f32),
            pltpu.VMEM((cols, 8, samples), f32),
            dma((2 + LOADS,)),
            pairs, pairs, pairs, pairs,
            dma((4, groups * halves)),
            dma((4, groups * col_tiles * PIECES)),
            dma((2, rows)),
            dma((2, cols)),
        ],
        compiler_params=pltpu.CompilerParams(
            collective_id=0, has_side_effects=True, vmem_limit_bytes=60 * 2**20
        ),
    )(tile_coords.T, tile_counts, alpha_now.reshape(1, samples), sens_tiles, data_vec, cell_vec)
    return data_next, cell_next, beta.reshape(samples), alpha.reshape(samples)


def solution(mesh):
    placed = (
        P(("blocks", "rows"), "cols", None),
        P(("blocks", "rows"), "cols"),
        P(("blocks", "rows"), "cols"),
        P("blocks", "rows"),
        P("blocks", "cols"),
        P("blocks"),
    )
    return jax.shard_map(
        functools.partial(per_device, mesh.shape["rows"], mesh.shape["cols"]),
        mesh=mesh,
        in_specs=placed,
        out_specs=(P("blocks", "rows"), P("blocks", "cols"), P("blocks"), P("blocks")),
        check_vma=False,
    )
```

time: 58.8 us -> 51.6 us (0.88)
  Pallas kernels: 50 us -> 45.2 us
  local copies, waits for them, and re-layouts: 7.27 us -> 4.86 us
    pallas_call x1, Pallas kernels: 50 us -> 45.2 us  [per_device(): pl.pallas_call(functools.partial(kernel, rows, cols, groups), out_shape=(...]
    unnamed x9 -> x8, local copies, waits for them, and re-layouts: 6.1 us -> 4.86 us
    reshape x1 -> x0, local copies, waits for them, and re-layouts: 0.66 us -> none  [per_device(): alpha_wide = jnp.pad(alpha_now, (0, lanes - samples)).reshape(1, lanes)]
where the time goes in v2:
time: 51.6 us; the launch traced here: 51.3 us
  Pallas kernels  45.2 us (88%)
  local copies, waits for them, and re-layouts  4.86 us (9%)
  between operations  1.3 us (3%)
    pallas_call x1, Pallas kernels, per_device(): pl.pallas_call(functools.partial(kernel, rows, cols, groups), out_shape=(...  45.2 us
    unnamed x8, local copies, waits for them, and re-layouts  4.86 us

profile of v2, /device:TPU:0, one launch (start us, length us, event | category | flops | bytes accessed | tf_op | source)
XLA Modules:
  0.0 51.3 jit_solution(11592271960773572827)
XLA Ops:
  1.3 45.2 %shard_map.93 = (f32[96,1024]{1,0:T(8,128)}, f32[96,2048]{1,0:T(8,128)}, f32[1,96]{1,0:T(1,128)}, f32[1,96]{1,0:T(1,128)}) custom-call(s32[2,16]{1,0:T(2,128)} %bitcast.4, s32[1,1]{1,0:T(1,128)S(6)} %copy.14.counts, f32[1,96]{1,0:T(1,128)} %bitcast.5, bf16[16,256,256]{2,1,0:T(8,128)(2,1)} %tiles_in.1, f32[96,1024]{1,0:T(8,128)} %data_in.1, f32[96,2048]{1,0:T(8,128)} %cell_in.1), custom_call_target="tpu_custom_call" | custom-call | tf_op jit(solution)/shard_map/pallas_call | solution.py:406
  46.5 0.0 copy-start.1
  46.5 0.0 copy-start
  46.5 1.8 %copy.15 = f32[96,1024]{1,0:T(8,128)} copy(f32[96,1024]{1,0:T(8,128)} %get-tuple-element.16) | data formatting | bytes 786432
  48.3 2.1 %copy.16 = f32[96,2048]{1,0:T(8,128)} copy(f32[96,2048]{1,0:T(8,128)} %get-tuple-element.17) | data formatting | bytes 1572864
  50.3 0.0 copy-done.1
  50.3 0.5 copy.17
  50.8 0.0 copy-done
  50.8 0.5 copy.18
Async XLA Ops:
  46.5 3.9 %copy-start.1 = (f32[1,96]{1,0:T(1,128)S(1)}, f32[1,96]{1,0:T(1,128)}, u32[]{:S(2)}) copy-start(f32[1,96]{1,0:T(1,128)} %get-tuple-element.10) | copy-start | bytes 1156
  46.5 4.4 %copy-start = (f32[1,96]{1,0:T(1,128)S(1)}, f32[1,96]{1,0:T(1,128)}, u32[]{:S(2)}) copy-start(f32[1,96]{1,0:T(1,128)} %get-tuple-element.11) | copy-start | bytes 1156

commit v3 on v2

--- a/solution.py
+++ b/solution.py
@@ -65,7 +65,7 @@
             def _():
                 if self.window:
 
-                    @pl.when(first)
+                    @pl.when(first & (i >= self.window))
                     def _():
                         self.paced(self.up_copy, i)
                         self.up_copy(self.own, i).start()
@@ -86,7 +86,7 @@
             def _():
                 if self.window:
 
-                    @pl.when(last)
+                    @pl.when(last & (k >= self.window))
                     def _():
                         self.paced(self.down_copy, k)
                         self.down_copy(self.own, k).start()
@@ -174,7 +174,7 @@
 def kernel(
     rows, cols, groups,
     coords, counts, alpha_in, tiles_in, data_in, cell_in,
-    data_out, cell_out, beta_out, alpha_out,
+    data_out, cell_out, norms_out,
     table, tiles, data, cell, cell_low, other, other_got, half, half_up, half_down, half_up_out, half_down_out,
     resid, part, part_up, part_down, part_up_out, part_down_out, squares, data_squares, beta_wide, inverse_wide,
     beta_row, beta_got, alpha_row, alpha_got,
@@ -322,7 +322,10 @@
                 term = jnp.dot(low[a], tiles[table[a * col_tiles + b]], preferred_element_type=jnp.float32)
                 total = term if total is None else total + term
             for e in range(PIECES):
-                part[(g * col_tiles + b) * PIECES + e] = total[e * strip:(e + 1) * strip]
+                i = (g * col_tiles + b) * PIECES + e
+                part[i] = total[e * strip:(e + 1) * strip]
+                if i < WINDOW:
+                    along.begin(i)
 
     multiply(0)
     if groups > 1:
@@ -349,7 +352,7 @@
             beta = jnp.sqrt(
                 share_end("rows", rows, r, beta_row, beta_got, beta_sems.at[0], beta_sems.at[1]) / data_total + EPSILON
             )
-            beta_out[...] = beta
+            norms_out[0:1] = beta
             column = as_column(beta)
             beta_wide[...] = jnp.broadcast_to(column, beta_wide.shape)
             inverse_wide[...] = jnp.broadcast_to(1.0 / column, inverse_wide.shape)
@@ -368,8 +371,7 @@
     share_start("cols", cols, c, as_row(sums), alpha_row, alpha_got, alpha_sems.at[0], alpha_sems.at[1])
     for g in range(groups):
         for a in range(row_tiles):
-            inverse = inverse_wide[span(g), :1]
-            data_out[span(g), a * tile:(a + 1) * tile] = resid[g * row_tiles + a] * inverse
+            data_out[span(g), a * tile:(a + 1) * tile] = resid[g * row_tiles + a]
     for g in range(groups):
         for j in range(halves):
             pair_copy(g * halves + j).wait_send()
@@ -379,11 +381,7 @@
     alpha_next = jnp.sqrt(
         share_end("cols", cols, c, alpha_row, alpha_got, alpha_sems.at[0], alpha_sems.at[1]) / cell_total + EPSILON
     )
-    alpha_out[...] = alpha_next
-    alpha_inverse = 1.0 / as_column(alpha_next)
-    for b in range(col_tiles):
-        here = slice(b * tile, (b + 1) * tile)
-        cell_out[:, here] = cell_out[:, here] * alpha_inverse
+    norms_out[1:2] = alpha_next
 
 
 def per_device(rows, cols, sens_tiles, tile_coords, tile_counts, data_vec, cell_vec, alpha_now):
@@ -403,16 +401,15 @@
     vmem = pl.BlockSpec(memory_space=pltpu.VMEM)
     smem = pl.BlockSpec(memory_space=pltpu.SMEM)
     hbm = pl.BlockSpec(memory_space=pltpu.HBM)
-    data_next, cell_next, beta, alpha = pl.pallas_call(
+    data_next, cell_next, norms = pl.pallas_call(
         functools.partial(kernel, rows, cols, groups),
         out_shape=(
             jax.ShapeDtypeStruct((samples, data_size), f32),
             jax.ShapeDtypeStruct((samples, cell_size), f32),
-            jax.ShapeDtypeStruct((1, samples), f32),
-            jax.ShapeDtypeStruct((1, samples), f32),
+            jax.ShapeDtypeStruct((2, samples), f32),
         ),
         in_specs=[smem, smem, vmem, hbm, hbm, hbm],
-        out_specs=(vmem, vmem, vmem, vmem),
+        out_specs=(vmem, vmem, vmem),
         scratch_shapes=[
             pltpu.SMEM((row_tiles * col_tiles,), jnp.int32),
             pltpu.VMEM((slots + 1, tile, tile), bf16),
@@ -435,10 +432,11 @@
             dma((2, cols)),
         ],
         compiler_params=pltpu.CompilerParams(
-            collective_id=0, has_side_effects=True, vmem_limit_bytes=60 * 2**20
+            collective_id=0, has_side_effects=True, vmem_limit_bytes=52 * 2**20
         ),
     )(tile_coords.T, tile_counts, alpha_now.reshape(1, samples), sens_tiles, data_vec, cell_vec)
-    return data_next, cell_next, beta.reshape(samples), alpha.reshape(samples)
+    beta, alpha = norms[0], norms[1]
+    return data_next / beta[:, None], cell_next / alpha[:, None], beta, alpha
 
 
 def solution(mesh):

time: 51.6 us -> 49.3 us (0.955)
  local copies, waits for them, and re-layouts: 4.86 us -> 2.34 us
  other arithmetic: 0 us -> 1.86 us
  Pallas kernels: 45.2 us -> 43.5 us
    unnamed x8 -> x10, local copies, waits for them, and re-layouts: 4.86 us -> 2.34 us
    div x0 -> x2, other arithmetic: none -> 1.86 us  [per_device(): return (data_next / beta[:, None], cell_next / alpha[:, None], beta, alpha)]
    pallas_call x1, Pallas kernels: 45.2 us -> 43.5 us  [per_device(): pl.pallas_call(functools.partial(kernel, rows, cols, groups), out_shape=(...]
where the time goes in v3:
time: 49.3 us; the launch traced here: 49 us
  Pallas kernels  43.5 us (88%)
  local copies, waits for them, and re-layouts  2.34 us (5%)
  other arithmetic  1.86 us (4%)
  between operations  1.32 us (3%)
    pallas_call x1, Pallas kernels, per_device(): pl.pallas_call(functools.partial(kernel, rows, cols, groups), out_shape=(...  43.5 us
    unnamed x10, local copies, waits for them, and re-layouts  2.34 us
    div x2, other arithmetic, per_device(): return (data_next / beta[:, None], cell_next / alpha[:, None], beta, alpha)  1.86 us

profile of v3, /device:TPU:0, one launch (start us, length us, event | category | flops | bytes accessed | tf_op | source)
XLA Modules:
  0.0 49.0 jit_solution(2254249170822263108)
XLA Ops:
  1.3 0.0 copy-start
  1.3 1.0 %copy-done = f32[96,1024]{1,0:T(8,128)S(1)} copy-done((f32[96,1024]{1,0:T(8,128)S(1)}, f32[96,1024]{1,0:T(8,128)}, u32[]{:S(2)}) %copy-start) | copy-done | bytes 393240
  2.3 0.0 copy-start.1
  2.3 0.7 %copy-done.1 = s32[16,2]{0,1:T(2,128)S(1)} copy-done((s32[16,2]{0,1:T(2,128)S(1)}, s32[16,2]{0,1:T(2,128)}, u32[]{:S(2)}) %copy-start.1) | copy-done | bytes 152
  3.0 0.0 copy-start.2
  3.0 0.7 %copy-done.2 = f32[96]{0:T(128)S(1)} copy-done((f32[96]{0:T(128)S(1)}, f32[96]{0:T(128)}, u32[]{:S(2)}) %copy-start.2) | copy-done | bytes 408
  3.6 43.5 %shard_map.93 = (f32[96,1024]{1,0:T(8,128)S(1)}, f32[96,2048]{1,0:T(8,128)S(1)}, f32[2,96]{1,0:T(2,128)S(1)}) custom-call(s32[2,16]{1,0:T(2,128)S(1)} %bitcast.6, s32[1,1]{1,0:T(1,128)S(6)} %copy.10.counts, f32[1,96]{1,0:T(1,128)S(1)} %bitcast.7, bf16[16,256,256]{2,1,0:T(8,128)(2,1)} %tiles_in.1, f32[96,1024]{1,0:T(8,128)S(1)} %copy-done, f32[96,2048]{1,0:T(8,128)} %cell_in.1), custom_call_target="tpu_custom_call" | custom-call | tf_op jit(solution)/shard_map/pallas_call | solution.py:404
  47.1 0.0 copy-start.3
  47.2 0.0 copy-start.4
  47.2 1.0 %broadcast_divide_fusion = f32[96,2048]{1,0:T(8,128)} fusion(f32[96,2048]{1,0:T(8,128)S(1)} %get-tuple-element.9, f32[96]{0:T(128)S(1)} %get-tuple-element.10), kind=kLoop, calls=%fused_computation | loop fusion | flops 196608 | bytes 1573248 | tf_op jit(solution)/shard_map/div | solution.py:439
  48.2 0.8 %broadcast_divide_fusion.1 = f32[96,1024]{1,0:T(8,128)} fusion(f32[96,1024]{1,0:T(8,128)S(1)} %get-tuple-element.7, f32[96]{0:T(128)S(1)} %get-tuple-element.11), kind=kLoop, calls=%fused_computation.1 | loop fusion | flops 98304 | bytes 786816 | tf_op jit(solution)/shard_map/div | solution.py:439
  49.0 0.0 copy-done.3
  49.0 0.0 copy-done.4
  (1 shorter events, 0.0 us)
Async XLA Ops:
  1.3 1.0 %copy-start = (f32[96,1024]{1,0:T(8,128)S(1)}, f32[96,1024]{1,0:T(8,128)}, u32[]{:S(2)}) copy-start(f32[96,1024]{1,0:T(8,128)} %data_in.1) | copy-start | bytes 1179652
  2.3 0.7 %copy-start.1 = (s32[16,2]{0,1:T(2,128)S(1)}, s32[16,2]{0,1:T(2,128)}, u32[]{:S(2)}) copy-start(s32[16,2]{0,1:T(2,128)} %param.7) | copy-start | bytes 388
  3.0 0.7 %copy-start.2 = (f32[96]{0:T(128)S(1)}, f32[96]{0:T(128)}, u32[]{:S(2)}) copy-start(f32[96]{0:T(128)} %param.11) | copy-start | bytes 1156
  47.1 1.9 %copy-start.3 = (f32[96]{0:T(128)}, f32[96]{0:T(128)S(1)}, u32[]{:S(2)}) copy-start(f32[96]{0:T(128)S(1)} %get-tuple-element.10) | copy-start | bytes 1156
  47.2 1.9 %copy-start.4 = (f32[96]{0:T(128)}, f32[96]{0:T(128)S(1)}, u32[]{:S(2)}) copy-start(f32[96]{0:T(128)S(1)} %get-tuple-element.11) | copy-start | bytes 1156
